TPU v7x, 32 devices: a whole 2x2x4 slice. The times are simulated.
32 devices in a mesh: tm: 8 (over y, x, core), tensor: 4 (over z).
Axes of the slice: x: 2, y: 2, z: 4, core: 2. Of those that a mesh axis runs over, the one named last changes fastest.
Arguments:
- latents: float32 [8, 1024, 3072], P('tm', None, 'tensor'), may hold values from -104 to 104
- noise: bfloat16 [8, 1024, 3072], P('tm', None, 'tensor'), may hold values from -5 to 5
- qkv_weight: bfloat16 [3072, 3, 3072], P(None, None, 'tensor'), may hold values from -0.108253175 to 0.108253175
- qk_gains: float32 [2, 3072], P(None, 'tensor'), may hold values from 0.45 to 6.6
- out_weight: bfloat16 [3072, 3072], P('tensor'), may hold values from -0.109375 to 0.109375
- modulation: bfloat16 [64, 3, 3072], P(None, None, 'tensor'), may hold values from -3 to 3
- step_sizes: float32 [64], replicated, may hold values from 0.02 to 0.08
- window_start: int32 [1], replicated, may hold values from 0 to 56
Outputs:
- updated: float32 [8, 1024, 3072], P('tm', None, 'tensor')
- velocity_out: bfloat16 [8, 1024, 3072], P('tm', None, 'tensor')
- slot_errors: float32 [8], P('tm')
All inputs are finite; a program needn't handle non-finite values.
Results may differ from a plain program's by a relative error of at most 0.012.
Values may be sent and summed in bfloat16 or wider, within the bound.
A program may use at most 192 MiB of HBM per device.

v0:
```python
import math

import jax
import jax.numpy as jnp
from jax import lax
from jax.sharding import PartitionSpec as P

HEAD = 128


epsilon = 1e-06


def entering(shard, axis, join, neutral):
    place = lax.axis_index(axis)
    gathered = lax.all_gather(shard.astype(jnp.bfloat16), axis)
    state = jnp.zeros_like(shard) + jnp.asarray(neutral, shard.dtype)

    def one(step, state):
        return join(state, lax.dynamic_index_in_dim(gathered, step, 0, False).astype(shard.dtype))

    return lax.fori_loop(0, place, one, state)


def rms_scale(vectors, gain_rows):
    power = jnp.mean(vectors * vectors, axis=-1, keepdims=True)
    return vectors * lax.rsqrt(power + epsilon) * gain_rows


def add_terms(earlier, later):
    return earlier + later


def body(latents, noise, qkv_weight, qk_gains, out_weight, modulation, step_sizes, window_start):
    slot_index = lax.axis_index("tm")
    offset = window_start[0] + slot_index
    mod_row = lax.dynamic_index_in_dim(modulation, offset, 0, keepdims=False)
    step_size = lax.dynamic_index_in_dim(step_sizes, offset, 0, keepdims=False)
    own_rows = latents[0]
    length = own_rows.shape[0]
    local_width = own_rows.shape[1]
    width = local_width * lax.axis_size("tensor")
    gathered, shift_rows = (
        lax.all_gather(own_rows.astype(jnp.bfloat16), "tensor", axis=1, tiled=True).astype(
            own_rows.dtype
        ),
        lax.all_gather(
            mod_row[:2].astype(jnp.float32).astype(jnp.bfloat16), "tensor", axis=1, tiled=True
        ).astype(jnp.float32),
    )
    row_mean = jnp.mean(gathered, axis=1, keepdims=True)
    row_var = jnp.mean(gathered * gathered, axis=1, keepdims=True) - row_mean * row_mean
    modulated = (
        (gathered - row_mean) * lax.rsqrt(row_var + epsilon) * (1.0 + shift_rows[1]) + shift_rows[0]
    ).astype(jnp.bfloat16)
    heads_dev = qkv_weight.shape[2] // HEAD
    projected = jnp.dot(
        modulated,
        qkv_weight.reshape(width, 3 * heads_dev * HEAD),
        preferred_element_type=jnp.float32,
    )
    projected = projected.reshape(length, 3, heads_dev, HEAD)
    gain_rows = qk_gains.reshape(2, heads_dev, HEAD)
    queries = rms_scale(projected[:, 0], gain_rows[0]).astype(jnp.bfloat16)
    keys_normed = rms_scale(projected[:, 1], gain_rows[1]).astype(jnp.bfloat16)
    values_heads = projected[:, 2].astype(jnp.bfloat16)
    scores = jnp.einsum(
        "qhd,khd->hqk", queries, keys_normed, preferred_element_type=jnp.float32
    ) * (1.0 / math.sqrt(HEAD))
    score_max = jnp.max(scores, axis=-1, keepdims=True)
    exp_scores = jnp.exp(scores - score_max)
    attn_weights = (exp_scores / jnp.sum(exp_scores, axis=-1, keepdims=True)).astype(jnp.bfloat16)
    attended = jnp.einsum(
        "hqk,khd->qhd", attn_weights, values_heads, preferred_element_type=jnp.float32
    )
    attended = attended.astype(jnp.bfloat16).reshape(length, heads_dev * HEAD)
    partials = jnp.dot(attended, out_weight, preferred_element_type=jnp.float32)
    branch = lax.psum_scatter(
        partials.astype(jnp.bfloat16), "tensor", scatter_dimension=1, tiled=True
    ).astype(jnp.float32)
    velocity = own_rows + mod_row[2].astype(jnp.float32) * branch
    increment = -step_size * velocity + noise[0].astype(jnp.float32)
    is_first = slot_index == 0
    scan_terms = increment + jnp.where(is_first, own_rows, 0.0)
    carried_sum = entering(scan_terms, "tm", add_terms, jnp.zeros_like(scan_terms))
    updated = jnp.where(is_first, own_rows, carried_sum)
    change = updated - own_rows
    slot_err = lax.psum(jnp.sum(change * change), "tensor") / (length * width)
    return (updated[None], velocity.astype(jnp.bfloat16)[None], slot_err.reshape(1))


def solution(mesh):
    return jax.shard_map(
        body,
        mesh=mesh,
        in_specs=(
            P("tm", None, "tensor"),
            P("tm", None, "tensor"),
            P(None, None, "tensor"),
            P(None, "tensor"),
            P("tensor", None),
            P(None, None, "tensor"),
            P(),
            P(),
        ),
        out_specs=(P("tm", None, "tensor"), P("tm", None, "tensor"), P("tm")),
        check_vma=False,
    )
```

profile of v0, /device:TPU:7, one launch (start us, length us, event | category | flops | bytes accessed | tf_op | source)
XLA Modules:
  0.0 410.7 jit_solution(13256848580091394070)
XLA Ops:
  7.2 0.0 all-gather.5.cloned.1.call-start
  7.2 3.2 bitcast_convert_fusion
  10.4 0.0 all-gather.5.cloned.1.call-update
  10.4 0.0 reduce-scatter.2.cloned.1.call-start
  11.1 0.8 constant_dynamic-slice_fusion
  11.9 10.7 %all-gather = bf16[1,2,3072]{2,0,1:T(2,128)(2,1)S(1)} all-gather(bf16[1,2,768]{2,0,1:T(2,128)(2,1)S(1)} %constant_dynamic-slice_fusion), channel_id=2, replica_groups=mesh['tm'=8,'tensor'=4] {'tensor'}, dimensions={2}, use_global_device_ids=true | all-gather | bytes 15360 | tf_op jit(solution)/shard_map/all_gather | solution.py:47
  22.6 0.0 copy-start.3
  22.6 18.8 %copy.14 = bf16[3072,3,768]{0,2,1:T(8,128)(2,1)} copy(bf16[3072,3,768]{2,0,1:T(8,128)(2,1)} %param.12) | data formatting | bytes 28311552 | tf_op args[2]
  41.4 0.0 copy-done.3
  41.5 85.9 %all-gather.5.cloned.1.call-done = bf16[1024,3072]{1,0:T(8,128)(2,1)} async-done(((bf16[1024,768]{1,0:T(8,128)(2,1)}), bf16[1024,3072]{1,0:T(8,128)(2,1)}) %all-gather.5.cloned.1.call-update) | async-done | bytes 6291472 | tf_op jit(solution)/shard_map/all_gather | solution.py:44
  127.4 0.0 copy-start.1
  127.4 4.8 %convert_reduce_fusion = (f32[1024]{0:T(1024)S(1)}, f32[1024]{0:T(1024)S(1)}) fusion(bf16[1024,3072]{1,0:T(8,128)(2,1)} %all-gather.5.cloned.1.call-done), kind=kLoop, calls=%fused_computation.8 | loop fusion | flops 12580864 | bytes 6299648 | tf_op jit(solution)/shard_map/reduce_sum | solution.py:51
  132.2 0.0 copy-done.1
  132.2 18.8 %fusion.12 = f32[1024,3,6,128]{0,3,2,1:T(8,128)S(1)} fusion(bf16[3,6,128,3072]{3,2,1,0:T(8,128)(2,1)} %bitcast.92, bf16[1024,3072]{1,0:T(8,128)(2,1)S(1)} %copy-done.1, f32[3072]{0:T(1024)S(1)} %bitcast.94, f32[3072]{0:T(1024)S(1)} %bitcast.95, f32[1024]{0:T(1024)S(1)} %get-tuple-element.46, f32[1024]{0:T(1024)S(1)} %get-tuple-element.45), kind=kOutput, calls=%fused_computation.17 | convolution fusion | flops 14514388992 | bytes 29917184 | tf_op jit(solution)/shard_map/dot_general | solution.py:57
  151.0 0.0 copy-start.2
  151.0 3.6 copy-done.2
  154.6 0.8 multiply_reduce_fusion.1
  155.5 0.0 slice-start
  155.5 14.5 %fusion.33 = (f32[6,1024]{1,0:T(8,128)S(1)}, f32[6,1024,1024]{1,2,0:T(8,128)}) fusion(f32[1024,3,6,128]{0,3,2,1:T(8,128)} %copy-done.2, f32[6,128]{1,0:T(8,128)S(1)} %bitcast.97, f32[1024,6]{0,1:T(8,128)S(1)} %get-tuple-element.50, f32[6,128]{1,0:T(8,128)S(1)} %bitcast.96, f32[1024,6]{0,1:T(8,128)S(1)} %get-tuple-element.49), kind=kOutput, calls=%fused_computation.58 | convolution fusion | flops 1634206720 | bytes 31537152 | tf_op jit(solution)/shard_map/sub | solution.py:71
  170.0 0.0 slice-start.1
  170.0 11.1 %fusion.26 = bf16[6,128,1024]{2,1,0:T(8,128)(2,1)S(1)} fusion(f32[6,1024,1024]{1,2,0:T(8,128)} %get-tuple-element.48, f32[6,1024]{1,0:T(8,128)S(1)} %get-tuple-element.47, f32[1024,3,6,128]{0,3,2,1:T(8,128)} %copy-done.2), kind=kOutput, calls=%fused_computation.43 | convolution fusion | flops 1623982080 | bytes 28336128 | tf_op jit(solution)/shard_map/hqk,khd->qhd/dot_general | solution.py:73
  181.1 0.0 slice-done
  181.1 0.0 slice-done.1
  181.2 7.1 %convolution_convert_fusion = bf16[1024,3072]{1,0:T(8,128)(2,1)} fusion(bf16[1024,768]{0,1:T(8,128)(2,1)S(1)} %bitcast.100, bf16[768,3072]{1,0:T(8,128)(2,1)S(1)} %bitcast.99), kind=kOutput, calls=%fused_computation.22 | convolution fusion | flops 4834983936 | bytes 12582912 | tf_op jit(solution)/shard_map/dot_general | solution.py:77
  188.3 0.0 copy-start.4
  188.3 0.0 copy-start
  188.3 0.0 reduce-scatter.2.cloned.1.call-update
  188.3 0.0 all-gather.7.cloned.1.call-start
  188.3 0.6 copy-done.4
  188.9 0.6 dynamic_slice.12
  190.1 0.7 fusion.31
  190.9 106.3 %reduce-scatter.2.cloned.1.call-done = bf16[1024,768]{1,0:T(8,128)(2,1)} async-done(((bf16[1024,3072]{1,0:T(8,128)(2,1)}), bf16[1024,768]{1,0:T(8,128)(2,1)}) %reduce-scatter.2.cloned.1.call-update) | async-done | bytes 1572880 | tf_op jit(solution)/shard_map/reduce_scatter | solution.py:78
  297.2 0.0 copy-done
  297.2 4.5 %fusion.27 = (bf16[1,1024,768]{2,1,0:T(8,128)(2,1)}, bf16[1024,768]{1,0:T(8,128)(2,1)}) fusion(bf16[1024,768]{1,0:T(8,128)(2,1)} %reduce-scatter.2.cloned.1.call-done, f32[1,1024,768]{2,1,0:T(8,128)S(1)} %copy-done, f32[768]{0:T(1024)S(1)} %fusion.31, pred[]{:T(512)S(6)} %eq.3, bf16[1,1024,768]{2,1,0:T(8,128)(2,1)} %param.11, f32[]{:T(128)} %bitcast.3), kind=kLoop, calls=%fused_computation.44 | loop fusion | flops 7864320 | bytes 9440261 | tf_op jit(solution)/shard_map/broadcast_in_dim | solution.py:89
  301.7 0.0 all-gather.7.cloned.1.call-update
  301.7 72.2 %all-gather.7.cloned.1.call-done = bf16[8192,768]{1,0:T(8,128)(2,1)} async-done(((bf16[1024,768]{1,0:T(8,128)(2,1)}), bf16[8192,768]{1,0:T(8,128)(2,1)}) %all-gather.7.cloned.1.call-update) | async-done | bytes 12582928 | tf_op jit(solution)/shard_map/all_gather | solution.py:16
  373.9 0.2 broadcast_in_dim.7
  374.1 12.9 %while.10 = (s32[]{:T(128)}, f32[1024,768]{1,0:T(8,128)S(1)}, s32[]{:T(128)}, bf16[8,1024,768]{2,1,0:T(8,128)(2,1)}, s32[]{:T(128)}, /*index=5*/s32[]{:T(128)}, s32[]{:T(128)}) while((s32[]{:T(128)}, f32[1024,768]{1,0:T(8,128)S(1)}, s32[]{:T(128)}, bf16[8,1024,768]{2,1,0:T(8,128)(2,1)}, s32[]{:T(128)}, /*index=5*/s32[]{:T(128)}, ...), condition=%wide.region_8.9_spmd, body=%wide.region_7.8_spmd.sunk | while | flops 1572869 | bytes 7864435 | solution.py:22
  374.2 1.8 convert_add_fusion.3
  376.0 1.8 convert_add_fusion.3
  377.9 1.8 convert_add_fusion.3
  379.7 1.8 convert_add_fusion.3
  381.6 1.8 convert_add_fusion.3
  383.4 1.8 convert_add_fusion.3
  385.2 1.8 convert_add_fusion.3
  387.1 5.0 %fusion.21 = (f32[]{:T(128)}, f32[1,1024,768]{2,1,0:T(8,128)}) fusion(f32[1,1024,768]{2,1,0:T(8,128)} %param.10, f32[1024,768]{1,0:T(8,128)S(1)} %get-tuple-element.26, pred[]{:T(512)S(6)} %eq.3), kind=kLoop, calls=%fused_computation.35 | loop fusion | flops 3145727 | bytes 9437189 | tf_op jit(solution)/shard_map/reduce_sum | solution.py:88
  392.0 10.3 %psum.7 = f32[]{:T(128)} all-reduce(f32[]{:T(128)} %get-tuple-element.41), channel_id=1, replica_groups=mesh['tm'=8,'tensor'=4] {'tensor'}, use_global_device_ids=true, to_apply=%region_10.11 | all-reduce | flops 1 | bytes 8 | tf_op jit(solution)/shard_map/psum | solution.py:88
  (7 shorter events, 0.1 us)
Async XLA Ops:
  7.2 120.2 %all-gather.5.cloned.1.call-start = ((), (), s32[]{:S(2)}) async-start(), calls=%async_computation.1 | async-start | bytes 7864320 | tf_op jit(solution)/shard_map/all_gather | solution.py:44
  10.4 286.8 %reduce-scatter.2.cloned.1.call-start = ((), (), s32[]{:S(2)}) async-start(), calls=%async_computation.2 | async-start | bytes 7864320 | tf_op jit(solution)/shard_map/reduce_scatter | solution.py:78
  22.6 18.8 %copy-start.3 = (f32[2,768]{1,0:T(2,128)S(1)}, f32[2,768]{1,0:T(2,128)}, u32[]{:S(2)}) copy-start(f32[2,768]{1,0:T(2,128)} %param.13) | copy-start | bytes 18436
  127.4 4.8 %copy-start.1 = (bf16[1024,3072]{1,0:T(8,128)(2,1)S(1)}, bf16[1024,3072]{1,0:T(8,128)(2,1)}, u32[]{:S(2)}) copy-start(bf16[1024,3072]{1,0:T(8,128)(2,1)} %all-gather.5.cloned.1.call-done) | copy-start | bytes 18874372
  151.0 3.6 copy-start.2
  155.5 25.7 %slice-start = ((s8[4718592]{0:T(1024)(128)(4,1)}), s8[524288]{0:T(1024)(128)(4,1)S(1)}, s32[]{:S(2)}) async-start(s8[4718592]{0:T(1024)(128)(4,1)} %bitcast.98), calls=%async_computation.4 | async-start | bytes 1048576
  170.0 11.1 %slice-start.1 = ((s8[4718592]{0:T(1024)(128)(4,1)}), s8[4194304]{0:T(1024)(128)(4,1)S(1)}, s32[]{:S(2)}) async-start(s8[4718592]{0:T(1024)(128)(4,1)} %bitcast.98), calls=%async_computation.5 | async-start | bytes 8388608
  188.3 0.7 copy-start.4
  188.3 108.9 %copy-start = (f32[1,1024,768]{2,1,0:T(8,128)S(1)}, f32[1,1024,768]{2,1,0:T(8,128)}, u32[]{:S(2)}) copy-start(f32[1,1024,768]{2,1,0:T(8,128)} %param.10) | copy-start | bytes 9437188
  188.3 185.6 %all-gather.7.cloned.1.call-start = ((), (), s32[]{:S(2)}) async-start(), calls=%async_computation.3 | async-start | bytes 14155776 | tf_op jit(solution)/shard_map/all_gather | solution.py:16
Sparse Core Ops, SparseCore 0:
  10.5 116.7 all-gather.4
  188.4 108.7 reduce-scatter.1
  301.8 72.0 all-gather.6
where the time goes:
time: 412 us; the launch traced here: 411 us
  waiting for transfers between devices  265 us (64%)
  matrix products  51.6 us (13%)
  other arithmetic  31.8 us (8%)
  local copies, waits for them, and re-layouts  24.5 us (6%)
  blocking collectives  21 us (5%)
  between operations  17 us (4%)
    reduce_scatter x1, waiting for transfers between devices, body(): lax.psum_scatter(partials.astype(jnp.bfloat16), 'tensor', scatter_dimensi...  106 us
    all_gather x1, waiting for transfers between devices, body(): lax.all_gather(own_rows.astype(jnp.bfloat16), 'tensor', axis=1, tiled=True)  85.9 us
    all_gather x1, waiting for transfers between devices, entering(): gathered = lax.all_gather(shard.astype(jnp.bfloat16), axis)  72.2 us
    unnamed x15, local copies, waits for them, and re-layouts  22.9 us
    dot_general x1, matrix products, body(): jnp.dot(modulated, qkv_weight.reshape(width, 3 * heads_dev * HEAD), prefe...  18.8 us
    sub x1, matrix products, body(): exp_scores = jnp.exp(scores - score_max)  14.5 us
    add x7, other arithmetic, add_terms(): return earlier + later  12.7 us
    dot_general x1, matrix products, body(): jnp.einsum('hqk,khd->qhd', attn_weights, values_heads, preferred_element_...  11.1 us
  transfers between devices with their start and end apart: 3, of which 3 were waited for; matrix products, arithmetic and copies ran while one was open for 5% of the time, Pallas kernels for 0%

commit v1 on v0

v1 whole, which is shorter than its diff:
```python
import functools
import math

import jax
import jax.numpy as jnp
from jax import lax
from jax.experimental import pallas as pl
from jax.experimental.pallas import tpu as pltpu
from jax.sharding import PartitionSpec as P

HEAD = 128
HDR = 16
CHUNK = 256
epsilon = 1e-06
f32 = jnp.float32
bf16 = jnp.bfloat16


def kernel(
    n, tm_size, chunk,
    x_ref, noise_hbm, w_hbm, gains_ref, wo_hbm, mod_ref, step_ref,
    upd_ref, vel_ref, err_ref,
    gat, wbuf, wo, qkv, rbuf, tsend, trecv, noise, modb, att, erracc, ebuf,
    load_sem, ag_send, ag_recv, rs_send, rs_recv, t_send, t_recv, e_send, e_recv,
):
    z = lax.axis_index("tensor")
    slot = lax.axis_index("tm")
    length, width = x_ref.shape
    full = n * width
    nc = length // chunk
    heads = width // HEAD
    levels = tm_size.bit_length() - 1
    first = slot == 0

    loads = [
        pltpu.make_async_copy(
            w_hbm.at[j], wbuf.at[pl.ds(j * full, full)], load_sem.at[j]
        )
        for j in range(3)
    ]
    loads.append(pltpu.make_async_copy(wo_hbm, wo, load_sem.at[3]))
    loads.append(pltpu.make_async_copy(noise_hbm, noise, load_sem.at[4]))

    def crows(c, base=0):
        return pl.ds(pl.multiple_of(base + c * chunk, 16), chunk)

    partners = []
    for k in range(levels):
        bit = lax.rem(slot // (1 << k), 2)
        partners.append((slot + (1 - 2 * bit) * (1 << k), bit))

    barrier = pltpu.get_barrier_semaphore()
    for d in range(1, n):
        pl.semaphore_signal(
            barrier, inc=1, device_id={"tensor": lax.rem(z + d, n)},
            device_id_type=pl.DeviceIdType.MESH,
        )
    for partner, _ in partners:
        pl.semaphore_signal(
            barrier, inc=1, device_id={"tm": partner},
            device_id_type=pl.DeviceIdType.MESH,
        )

    gat[z, pl.ds(0, HDR), :] = mod_ref[...].astype(bf16)

    def cast(c, carry):
        gat[z, crows(c, HDR), :] = x_ref[crows(c), :].astype(bf16)
        return carry

    lax.fori_loop(0, nc, cast, 0)
    pl.semaphore_wait(barrier, n - 1 + levels)

    right = jnp.minimum(z + 1, n - 1)
    left = jnp.maximum(z - 1, 0)

    def ag(s, c, way):
        rows = pl.ds(0, HDR) if c is None else crows(c, HDR)
        i = nc if c is None else c
        return pltpu.make_async_remote_copy(
            src_ref=gat.at[s, rows], dst_ref=gat.at[s, rows],
            send_sem=ag_send.at[way, s, i], recv_sem=ag_recv.at[s, i],
            device_id={"tensor": right if way == 0 else left},
            device_id_type=pl.DeviceIdType.MESH,
        )

    def own(c):
        @pl.when(z < n - 1)
        def _():
            ag(z, c, 0).start()

        @pl.when(z > 0)
        def _():
            ag(z, c, 1).start()

    def forward(d, c):
        @pl.when(z >= d)
        def _():
            ag(z - d, c, 0).wait_recv()

            @pl.when(z < n - 1)
            def _():
                ag(z - d, c, 0).start()

        @pl.when(z + d < n)
        def _():
            ag(z + d, c, 1).wait_recv()

            @pl.when(z > 0)
            def _():
                ag(z + d, c, 1).start()

    own(None)

    def own_loop(c, carry):
        own(c)
        return carry

    lax.fori_loop(0, nc, own_loop, 0)
    for load in loads:
        load.start()

    for d in range(1, n):
        forward(d, None)
        if d < n - 1:

            def forward_loop(c, carry, d=d):
                forward(d, c)
                return carry

            lax.fori_loop(0, nc, forward_loop, 0)

    for load in loads:
        load.wait()

    def project(c, carry):
        forward(n - 1, c)
        rows = crows(c, HDR)
        total = jnp.zeros((chunk, 1), f32)
        square = jnp.zeros((chunk, 1), f32)
        for s in range(n):
            part = gat[s, rows, :].astype(f32)
            total += jnp.sum(part, axis=1, keepdims=True)
            square += jnp.sum(part * part, axis=1, keepdims=True)
        mean = total * (1.0 / full)
        var = square * (1.0 / full) - mean * mean
        rstd = lax.rsqrt(var + epsilon)
        for s in range(n):
            head_rows = gat[s, pl.ds(0, HDR), :].astype(f32)
            part = gat[s, rows, :].astype(f32)
            modb[:, s * width : (s + 1) * width] = (
                (part - mean) * rstd * (1.0 + head_rows[1:2]) + head_rows[0:1]
            ).astype(bf16)
        for j in range(3):
            out = jnp.dot(
                modb[...], wbuf[j * full : (j + 1) * full, :], preferred_element_type=f32
            )
            if j == 2:
                qkv[j, crows(c), :] = out.astype(bf16)
            else:
                for h in range(heads):
                    cols = slice(h * HEAD, (h + 1) * HEAD)
                    vec = out[:, cols]
                    power = jnp.mean(vec * vec, axis=1, keepdims=True)
                    qkv[j, crows(c), cols] = (
                        vec * lax.rsqrt(power + epsilon) * gains_ref[j : j + 1, cols]
                    ).astype(bf16)
        return carry

    lax.fori_loop(0, nc, project, 0)

    def prow(t, c):
        return pl.ds(pl.multiple_of(t * length + c * chunk, 16), chunk)

    def rs(t, c, way):
        if way == 0:
            place = t
        else:
            place = jnp.where(t == z - 1, n, t)
        return pltpu.make_async_remote_copy(
            src_ref=wbuf.at[prow(t, c)], dst_ref=rbuf.at[place, crows(c)],
            send_sem=rs_send.at[way, t, c], recv_sem=rs_recv.at[way, t, c],
            device_id={"tensor": right if way == 0 else left},
            device_id_type=pl.DeviceIdType.MESH,
        )

    def tx(k, c):
        return pltpu.make_async_remote_copy(
            src_ref=tsend.at[k, crows(c)], dst_ref=trecv.at[k, crows(c)],
            send_sem=t_send.at[k, c], recv_sem=t_recv.at[k, c],
            device_id={"tm": partners[k][0]}, device_id_type=pl.DeviceIdType.MESH,
        )

    exponent = math.log2(math.e) / math.sqrt(HEAD)

    def stage_attend(c):
        def one_head(h, carry):
            cols = pl.ds(pl.multiple_of(h * HEAD, HEAD), HEAD)
            scores = lax.dot_general(
                qkv[0, crows(c), cols], qkv[1, :, cols], (((1,), (1,)), ((), ())),
                preferred_element_type=f32,
            )
            top = jnp.max(scores, axis=1, keepdims=True)
            weights = jnp.exp2((scores - top) * exponent)
            norm = jnp.sum(weights, axis=1, keepdims=True)
            out = jnp.dot(weights.astype(bf16), qkv[2, :, cols], preferred_element_type=f32)
            att[:, cols] = (out / norm).astype(bf16)
            return carry

        lax.fori_loop(0, heads, one_head, 0, unroll=3)

        def one_part(t, carry):
            cols = pl.ds(pl.multiple_of(t * width, 128), width)
            part = jnp.dot(att[...], wo[:, cols], preferred_element_type=f32)
            wbuf[prow(t, c), :] = part.astype(bf16)
            return carry

        lax.fori_loop(0, n, one_part, 0)

        @pl.when(z == 0)
        def _():
            for t in range(n - 1, 0, -1):
                rs(t, c, 0).start()

        @pl.when(z == n - 1)
        def _():
            for t in range(n - 1):
                rs(t, c, 1).start()

    def stage_join(c):
        for t in range(n - 1, 0, -1):
            @pl.when((z > 0) & (z < t))
            def _():
                rs(t, c, 0).wait_recv()
                wbuf[prow(t, c), :] = (
                    wbuf[prow(t, c), :].astype(f32) + rbuf[t, crows(c), :].astype(f32)
                ).astype(bf16)
                rs(t, c, 0).start()

            u = n - 1 - t

            @pl.when((z < n - 1) & (z > u))
            def _():
                rs(u, c, 1).wait_recv()
                wbuf[prow(u, c), :] = (
                    wbuf[prow(u, c), :].astype(f32) + rbuf[u, crows(c), :].astype(f32)
                ).astype(bf16)
                rs(u, c, 1).start()

    def stage_velocity(c):
        rows = crows(c)

        @pl.when(z > 0)
        def _():
            rs(z, c, 0).wait_recv()

        @pl.when(z < n - 1)
        def _():
            pltpu.make_async_remote_copy(
                src_ref=wbuf.at[prow(z, c)], dst_ref=rbuf.at[n, rows],
                send_sem=rs_send.at[1, z, c], recv_sem=rs_recv.at[1, z, c],
                device_id={"tensor": right}, device_id_type=pl.DeviceIdType.MESH,
            ).wait_recv()

        branch = wbuf[prow(z, c), :].astype(f32)
        upd_ref[rows, :] = branch

        @pl.when(z > 0)
        def _():
            upd_ref[rows, :] = upd_ref[rows, :] + rbuf[z, rows, :].astype(f32)

        @pl.when(z < n - 1)
        def _():
            upd_ref[rows, :] = upd_ref[rows, :] + rbuf[n, rows, :].astype(f32)

        state = x_ref[rows, :]
        velocity = state + mod_ref[2:3, :] * upd_ref[rows, :]
        vel_ref[rows, :] = velocity.astype(bf16)
        start = jnp.where(first, state, jnp.zeros_like(state))
        upd_ref[rows, :] = start
        tsend[0, rows, :] = (
            noise[rows, :].astype(f32) - step_ref[0] * velocity + start
        ).astype(bf16)
        tx(0, c).start()

    def stage_prefix(k, c):
        rows = crows(c)
        tx(k, c).wait_recv()
        arrived = trecv[k, rows, :].astype(f32)
        if k < levels - 1:
            tsend[k + 1, rows, :] = (tsend[k, rows, :].astype(f32) + arrived).astype(bf16)
            tx(k + 1, c).start()
        keep = partners[k][1].astype(f32)
        now = upd_ref[rows, :] + keep * arrived
        upd_ref[rows, :] = now
        if k == levels - 1:
            change = now - x_ref[rows, :]
            erracc[...] += jnp.sum(
                (change * change).reshape(chunk // 8, 8, width), axis=0
            )

    erracc[...] = jnp.zeros_like(erracc)
    lag = 2

    def turn(i, carry):
        @pl.when(i < nc)
        def _():
            stage_attend(i)

        @pl.when((i >= 1) & (i < nc + 1))
        def _():
            stage_join(i - 1)

        @pl.when((i >= lag) & (i < nc + lag))
        def _():
            stage_velocity(i - lag)

        for k in range(levels):
            @pl.when((i >= lag + 1 + k) & (i < nc + lag + 1 + k))
            def _(k=k):
                stage_prefix(k, i - (lag + 1 + k))

        return carry

    lax.fori_loop(0, nc + lag + levels, turn, 0)

    ebuf[z] = jnp.zeros((8, 128), f32) + jnp.sum(erracc[...])

    def ex(d):
        return pltpu.make_async_remote_copy(
            src_ref=ebuf.at[z], dst_ref=ebuf.at[z],
            send_sem=e_send.at[d], recv_sem=e_recv.at[d],
            device_id={"tensor": lax.rem(z + d, n)}, device_id_type=pl.DeviceIdType.MESH,
        )

    for d in range(1, n):
        ex(d).start()

    def drain(c, carry):
        for s in range(n):
            @pl.when((z < n - 1) & (s <= z))
            def _():
                ag(s, c, 0).wait_send()

            @pl.when((z > 0) & (s >= z))
            def _():
                ag(s, c, 1).wait_send()

            @pl.when(z < s)
            def _():
                rs(s, c, 0).wait_send()

            @pl.when(z > s)
            def _():
                rs(s, c, 1).wait_send()

        for k in range(levels):
            tx(k, c).wait_send()
        return carry

    lax.fori_loop(0, nc, drain, 0)
    for s in range(n):
        @pl.when((z < n - 1) & (s <= z))
        def _():
            ag(s, None, 0).wait_send()

        @pl.when((z > 0) & (s >= z))
        def _():
            ag(s, None, 1).wait_send()

    for d in range(1, n):
        ex(d).wait()
    total = ebuf[0]
    for s in range(1, n):
        total = total + ebuf[s]
    err_ref[...] = total


def body(latents, noise, qkv_weight, qk_gains, out_weight, modulation, step_sizes, window_start):
    n = lax.axis_size("tensor")
    tm_size = lax.axis_size("tm")
    offset = window_start[0] + lax.axis_index("tm")
    _, length, width = latents.shape
    full = n * width
    mod_rows = lax.dynamic_index_in_dim(
        modulation.transpose(1, 0, 2), offset, 1, keepdims=False
    ).astype(f32)
    mod_rows = jnp.pad(mod_rows, ((0, HDR - 3), (0, 0)))
    step_size = lax.dynamic_slice_in_dim(step_sizes, offset, 1, 0)
    chunk = CHUNK
    nc = length // chunk
    levels = tm_size.bit_length() - 1
    vmem = pl.BlockSpec(memory_space=pltpu.VMEM)
    hbm = pl.BlockSpec(memory_space=pl.ANY)
    dma = pltpu.SemaphoreType.DMA
    updated, velocity, err = pl.pallas_call(
        functools.partial(kernel, n, tm_size, chunk),
        out_shape=(
            jax.ShapeDtypeStruct((length, width), f32),
            jax.ShapeDtypeStruct((length, width), bf16),
            jax.ShapeDtypeStruct((8, 128), f32),
        ),
        in_specs=[vmem, hbm, hbm, vmem, hbm, vmem, pl.BlockSpec(memory_space=pltpu.SMEM)],
        out_specs=(vmem, vmem, vmem),
        scratch_shapes=[
            pltpu.VMEM((n, HDR + length, width), bf16),
            pltpu.VMEM((3 * full, width), bf16),
            pltpu.VMEM((width, full), bf16),
            pltpu.VMEM((3, length, width), bf16),
            pltpu.VMEM((n + 1, length, width), bf16),
            pltpu.VMEM((levels, length, width), bf16),
            pltpu.VMEM((levels, length, width), bf16),
            pltpu.VMEM((length, width), bf16),
            pltpu.VMEM((chunk, full), bf16),
            pltpu.VMEM((chunk, width), bf16),
            pltpu.VMEM((8, width), f32),
            pltpu.VMEM((n, 8, 128), f32),
            dma((5,)),
            dma((2, n, nc + 1)),
            dma((n, nc + 1)),
            dma((2, n, nc)),
            dma((2, n, nc)),
            dma((levels, nc)),
            dma((levels, nc)),
            dma((n,)),
            dma((n,)),
        ],
        compiler_params=pltpu.CompilerParams(
            collective_id=0, has_side_effects=True, vmem_limit_bytes=62 * 2**20
        ),
    )(
        latents[0], noise[0], qkv_weight.transpose(1, 0, 2), qk_gains, out_weight,
        mod_rows, step_size,
    )
    return (updated[None], velocity[None], err[0, :1] / (length * full))


def solution(mesh):
    return jax.shard_map(
        body,
        mesh=mesh,
        in_specs=(
            P("tm", None, "tensor"),
            P("tm", None, "tensor"),
            P(None, None, "tensor"),
            P(None, "tensor"),
            P("tensor", None),
            P(None, None, "tensor"),
            P(),
            P(),
        ),
        out_specs=(P("tm", None, "tensor"), P("tm", None, "tensor"), P("tm")),
        check_vma=False,
    )
```

time: 412 us -> 283 us (0.69)
  the two profiles are of different devices: /device:TPU:7 before, /device:TPU:0 now
where the time goes in v1:
time: 283 us
  Pallas kernels  271 us (96%)
  local copies, waits for them, and re-layouts  7.48 us (3%)
  between operations  3.15 us (1%)
    pallas_call x1, Pallas kernels, body(): pl.pallas_call(functools.partial(kernel, n, tm_size, chunk), out_shape=(j...  271 us

profile of v1, /device:TPU:0, one launch (start us, length us, event | category | flops | bytes accessed | tf_op | source)
XLA Modules:
  0.0 282.7 jit_solution(10362507471631216034)
XLA Ops:
  0.6 0.0 copy-start
  1.3 1.2 dynamic_slice.5.step_ref
  2.6 0.0 copy-done
  2.6 0.6 pad_convert_fusion.mod_ref
  3.2 271.4 %shard_map.103 = (f32[1024,768]{1,0:T(8,128)}, bf16[1024,768]{1,0:T(8,128)(2,1)}, f32[8,128]{1,0:T(8,128)}) custom-call(f32[1024,768]{1,0:T(8,128)} %bitcast.13, bf16[1024,768]{1,0:T(8,128)(2,1)} %bitcast.15, bf16[3,3072,768]{2,1,0:T(8,128)(2,1)} %bitcast.11, f32[2,768]{1,0:T(2,128)} %gains_ref.1, bf16[768,3072]{1,0:T(8,128)(2,1)} %wo_hbm.1, ...), custom_call_target="tpu_custom_call" | custom-call | tf_op jit(solution)/shard_map/pallas_call | solution.py:395
  274.7 1.2 slice.3
  276.5 0.0 copy-start.1
  276.5 3.9 %copy.17 = f32[1,1024,768]{2,1,0:T(8,128)} copy(f32[1,1024,768]{2,1,0:T(8,128)} %bitcast.12) | data formatting | bytes 6291456
  280.4 0.0 copy-done.1
  280.4 1.1 copy.18
  (2 shorter events, 0.0 us)
Async XLA Ops:
  0.6 2.0 copy-start
  276.5 3.9 %copy-start.1 = (bf16[1024,768]{1,0:T(8,128)(2,1)S(1)}, bf16[1024,768]{1,0:T(8,128)(2,1)}, u32[]{:S(2)}) copy-start(bf16[1024,768]{1,0:T(8,128)(2,1)} %get-tuple-element.7) | copy-start | bytes 4718596

commit v2 on v1

--- a/solution.py
+++ b/solution.py
@@ -11,6 +11,7 @@
 HEAD = 128
 HDR = 16
 CHUNK = 256
+SPLIT = 2
 epsilon = 1e-06
 f32 = jnp.float32
 bf16 = jnp.bfloat16
@@ -21,13 +22,15 @@
     x_ref, noise_hbm, w_hbm, gains_ref, wo_hbm, mod_ref, step_ref,
     upd_ref, vel_ref, err_ref,
     gat, wbuf, wo, qkv, rbuf, tsend, trecv, noise, modb, att, erracc, ebuf,
-    load_sem, ag_send, ag_recv, rs_send, rs_recv, t_send, t_recv, e_send, e_recv,
+    load_sem, ag_send, ag_recv, rs_send, rs_recv, t_send, t_recv, e_send, e_recv, gate,
 ):
     z = lax.axis_index("tensor")
     slot = lax.axis_index("tm")
     length, width = x_ref.shape
     full = n * width
     nc = length // chunk
+    sub = chunk // SPLIT
+    ns = nc * SPLIT
     heads = width // HEAD
     levels = tm_size.bit_length() - 1
     first = slot == 0
@@ -43,6 +46,9 @@
 
     def crows(c, base=0):
         return pl.ds(pl.multiple_of(base + c * chunk, 16), chunk)
+
+    def srows(c):
+        return pl.ds(pl.multiple_of(c * sub, 16), sub)
 
     partners = []
     for k in range(levels):
@@ -109,6 +115,15 @@
             def _():
                 ag(z + d, c, 1).start()
 
+    for load in loads:
+        load.start()
+
+    even = partners[0][1] == 0
+
+    @pl.when(jnp.logical_not(even))
+    def _():
+        pl.semaphore_wait(gate, 1)
+
     own(None)
 
     def own_loop(c, carry):
@@ -116,8 +131,24 @@
         return carry
 
     lax.fori_loop(0, nc, own_loop, 0)
-    for load in loads:
-        load.start()
+
+    def drain_gather():
+        def one(c, carry):
+            drain_one(c)
+            return carry
+
+        drain_one(None)
+        lax.fori_loop(0, nc, one, 0)
+
+    def drain_one(c):
+        for s in range(n):
+            @pl.when((z < n - 1) & (s <= z))
+            def _():
+                ag(s, c, 0).wait_send()
+
+            @pl.when((z > 0) & (s >= z))
+            def _():
+                ag(s, c, 1).wait_send()
 
     for d in range(1, n):
         forward(d, None)
@@ -134,6 +165,15 @@
 
     def project(c, carry):
         forward(n - 1, c)
+
+        @pl.when((c == nc - 1) & even)
+        def _():
+            drain_gather()
+            pl.semaphore_signal(
+                gate, inc=1, device_id={"tm": partners[0][0]},
+                device_id_type=pl.DeviceIdType.MESH,
+            )
+
         rows = crows(c, HDR)
         total = jnp.zeros((chunk, 1), f32)
         square = jnp.zeros((chunk, 1), f32)
@@ -169,7 +209,7 @@
     lax.fori_loop(0, nc, project, 0)
 
     def prow(t, c):
-        return pl.ds(pl.multiple_of(t * length + c * chunk, 16), chunk)
+        return pl.ds(pl.multiple_of(t * length + c * sub, 16), sub)
 
     def rs(t, c, way):
         if way == 0:
@@ -177,7 +217,7 @@
         else:
             place = jnp.where(t == z - 1, n, t)
         return pltpu.make_async_remote_copy(
-            src_ref=wbuf.at[prow(t, c)], dst_ref=rbuf.at[place, crows(c)],
+            src_ref=wbuf.at[prow(t, c)], dst_ref=rbuf.at[place, srows(c)],
             send_sem=rs_send.at[way, t, c], recv_sem=rs_recv.at[way, t, c],
             device_id={"tensor": right if way == 0 else left},
             device_id_type=pl.DeviceIdType.MESH,
@@ -185,7 +225,7 @@
 
     def tx(k, c):
         return pltpu.make_async_remote_copy(
-            src_ref=tsend.at[k, crows(c)], dst_ref=trecv.at[k, crows(c)],
+            src_ref=tsend.at[k, srows(c)], dst_ref=trecv.at[k, srows(c)],
             send_sem=t_send.at[k, c], recv_sem=t_recv.at[k, c],
             device_id={"tm": partners[k][0]}, device_id_type=pl.DeviceIdType.MESH,
         )
@@ -211,20 +251,24 @@
         def one_part(t, carry):
             cols = pl.ds(pl.multiple_of(t * width, 128), width)
             part = jnp.dot(att[...], wo[:, cols], preferred_element_type=f32)
-            wbuf[prow(t, c), :] = part.astype(bf16)
+            wbuf[pl.ds(pl.multiple_of(t * length + c * chunk, 16), chunk), :] = part.astype(
+                bf16
+            )
             return carry
 
         lax.fori_loop(0, n, one_part, 0)
 
         @pl.when(z == 0)
         def _():
-            for t in range(n - 1, 0, -1):
-                rs(t, c, 0).start()
+            for p in range(SPLIT):
+                for t in range(n - 1, 0, -1):
+                    rs(t, c * SPLIT + p, 0).start()
 
         @pl.when(z == n - 1)
         def _():
-            for t in range(n - 1):
-                rs(t, c, 1).start()
+            for p in range(SPLIT):
+                for t in range(n - 1):
+                    rs(t, c * SPLIT + p, 1).start()
 
     def stage_join(c):
         for t in range(n - 1, 0, -1):
@@ -232,7 +276,7 @@
             def _():
                 rs(t, c, 0).wait_recv()
                 wbuf[prow(t, c), :] = (
-                    wbuf[prow(t, c), :].astype(f32) + rbuf[t, crows(c), :].astype(f32)
+                    wbuf[prow(t, c), :].astype(f32) + rbuf[t, srows(c), :].astype(f32)
                 ).astype(bf16)
                 rs(t, c, 0).start()
 
@@ -242,12 +286,12 @@
             def _():
                 rs(u, c, 1).wait_recv()
                 wbuf[prow(u, c), :] = (
-                    wbuf[prow(u, c), :].astype(f32) + rbuf[u, crows(c), :].astype(f32)
+                    wbuf[prow(u, c), :].astype(f32) + rbuf[u, srows(c), :].astype(f32)
                 ).astype(bf16)
                 rs(u, c, 1).start()
 
     def stage_velocity(c):
-        rows = crows(c)
+        rows = srows(c)
 
         @pl.when(z > 0)
         def _():
@@ -283,7 +327,7 @@
         tx(0, c).start()
 
     def stage_prefix(k, c):
-        rows = crows(c)
+        rows = srows(c)
         tx(k, c).wait_recv()
         arrived = trecv[k, rows, :].astype(f32)
         if k < levels - 1:
@@ -295,33 +339,33 @@
         if k == levels - 1:
             change = now - x_ref[rows, :]
             erracc[...] += jnp.sum(
-                (change * change).reshape(chunk // 8, 8, width), axis=0
+                (change * change).reshape(sub // 8, 8, width), axis=0
             )
 
     erracc[...] = jnp.zeros_like(erracc)
-    lag = 2
+    lag = 5
 
     def turn(i, carry):
-        @pl.when(i < nc)
-        def _():
-            stage_attend(i)
-
-        @pl.when((i >= 1) & (i < nc + 1))
+        @pl.when((i < ns) & (lax.rem(i, SPLIT) == 0))
+        def _():
+            stage_attend(i // SPLIT)
+
+        @pl.when((i >= 1) & (i < ns + 1))
         def _():
             stage_join(i - 1)
 
-        @pl.when((i >= lag) & (i < nc + lag))
+        @pl.when((i >= lag) & (i < ns + lag))
         def _():
             stage_velocity(i - lag)
 
         for k in range(levels):
-            @pl.when((i >= lag + 1 + k) & (i < nc + lag + 1 + k))
+            @pl.when((i >= lag + 1 + k) & (i < ns + lag + 1 + k))
             def _(k=k):
                 stage_prefix(k, i - (lag + 1 + k))
 
         return carry
 
-    lax.fori_loop(0, nc + lag + levels, turn, 0)
+    lax.fori_loop(0, ns + lag + levels, turn, 0)
 
     ebuf[z] = jnp.zeros((8, 128), f32) + jnp.sum(erracc[...])
 
@@ -335,16 +379,12 @@
     for d in range(1, n):
         ex(d).start()
 
+    @pl.when(jnp.logical_not(even))
+    def _():
+        drain_gather()
+
     def drain(c, carry):
         for s in range(n):
-            @pl.when((z < n - 1) & (s <= z))
-            def _():
-                ag(s, c, 0).wait_send()
-
-            @pl.when((z > 0) & (s >= z))
-            def _():
-                ag(s, c, 1).wait_send()
-
             @pl.when(z < s)
             def _():
                 rs(s, c, 0).wait_send()
@@ -357,16 +397,7 @@
             tx(k, c).wait_send()
         return carry
 
-    lax.fori_loop(0, nc, drain, 0)
-    for s in range(n):
-        @pl.when((z < n - 1) & (s <= z))
-        def _():
-            ag(s, None, 0).wait_send()
-
-        @pl.when((z > 0) & (s >= z))
-        def _():
-            ag(s, None, 1).wait_send()
-
+    lax.fori_loop(0, ns, drain, 0)
     for d in range(1, n):
         ex(d).wait()
     total = ebuf[0]
@@ -388,6 +419,7 @@
     step_size = lax.dynamic_slice_in_dim(step_sizes, offset, 1, 0)
     chunk = CHUNK
     nc = length // chunk
+    ns = nc * SPLIT
     levels = tm_size.bit_length() - 1
     vmem = pl.BlockSpec(memory_space=pltpu.VMEM)
     hbm = pl.BlockSpec(memory_space=pl.ANY)
@@ -417,12 +449,13 @@
             dma((5,)),
             dma((2, n, nc + 1)),
             dma((n, nc + 1)),
-            dma((2, n, nc)),
-            dma((2, n, nc)),
-            dma((levels, nc)),
-            dma((levels, nc)),
+            dma((2, n, ns)),
+            dma((2, n, ns)),
+            dma((levels, ns)),
+            dma((levels, ns)),
             dma((n,)),
             dma((n,)),
+            pltpu.SemaphoreType.REGULAR,
         ],
         compiler_params=pltpu.CompilerParams(
             collective_id=0, has_side_effects=True, vmem_limit_bytes=62 * 2**20

time: 283 us -> 283 us (level)
  no operation moved by 1% of the time
where the time goes in v2:
time: 283 us; the launch traced here: 282 us
  Pallas kernels  271 us (96%)
  local copies, waits for them, and re-layouts  7.48 us (3%)
  between operations  3.15 us (1%)
    pallas_call x1, Pallas kernels, body(): pl.pallas_call(functools.partial(kernel, n, tm_size, chunk), out_shape=(j...  271 us

profile of v2, /device:TPU:0, one launch (start us, length us, event | category | flops | bytes accessed | tf_op | source)
XLA Modules:
  0.0 282.4 jit_solution(2303823272251601891)
XLA Ops:
  0.6 0.0 copy-start
  1.3 1.2 dynamic_slice.5.step_ref
  2.6 0.0 copy-done
  2.6 0.6 pad_convert_fusion.mod_ref
  3.2 271.1 %shard_map.103 = (f32[1024,768]{1,0:T(8,128)}, bf16[1024,768]{1,0:T(8,128)(2,1)}, f32[8,128]{1,0:T(8,128)}) custom-call(f32[1024,768]{1,0:T(8,128)} %bitcast.13, bf16[1024,768]{1,0:T(8,128)(2,1)} %bitcast.15, bf16[3,3072,768]{2,1,0:T(8,128)(2,1)} %bitcast.11, f32[2,768]{1,0:T(2,128)} %gains_ref.1, bf16[768,3072]{1,0:T(8,128)(2,1)} %wo_hbm.1, ...), custom_call_target="tpu_custom_call" | custom-call | tf_op jit(solution)/shard_map/pallas_call | solution.py:427
  274.4 1.2 slice.3
  276.2 0.0 copy-start.1
  276.2 3.9 %copy.17 = f32[1,1024,768]{2,1,0:T(8,128)} copy(f32[1,1024,768]{2,1,0:T(8,128)} %bitcast.12) | data formatting | bytes 6291456
  280.1 0.0 copy-done.1
  280.1 1.1 copy.18
  (2 shorter events, 0.0 us)
Async XLA Ops:
  0.6 2.0 copy-start
  276.2 3.9 %copy-start.1 = (bf16[1024,768]{1,0:T(8,128)(2,1)S(1)}, bf16[1024,768]{1,0:T(8,128)(2,1)}, u32[]{:S(2)}) copy-start(bf16[1024,768]{1,0:T(8,128)(2,1)} %get-tuple-element.7) | copy-start | bytes 4718596

commit v3 on v2

--- a/solution.py
+++ b/solution.py
@@ -21,8 +21,9 @@
     n, tm_size, chunk,
     x_ref, noise_hbm, w_hbm, gains_ref, wo_hbm, mod_ref, step_ref,
     upd_ref, vel_ref, err_ref,
-    gat, wbuf, wo, qkv, rbuf, tsend, trecv, noise, modb, att, erracc, ebuf,
-    load_sem, ag_send, ag_recv, rs_send, rs_recv, t_send, t_recv, e_send, e_recv, gate,
+    gat, wbuf, wo, qkv, rbuf, trecv, noise, acc, att, erracc, ebuf, sums, stat,
+    load_sem, ag_send, ag_recv, rs_send, rs_recv, t_send, t_recv, e_send, e_recv,
+    s_send, s_recv, gate,
 ):
     z = lax.axis_index("tensor")
     slot = lax.axis_index("tm")
@@ -67,6 +68,9 @@
             device_id_type=pl.DeviceIdType.MESH,
         )
 
+    for load in loads:
+        load.start()
+
     gat[z, pl.ds(0, HDR), :] = mod_ref[...].astype(bf16)
 
     def cast(c, carry):
@@ -115,22 +119,49 @@
             def _():
                 ag(z + d, c, 1).start()
 
-    for load in loads:
-        load.start()
-
     even = partners[0][1] == 0
 
-    @pl.when(jnp.logical_not(even))
+    def own_all():
+        own(None)
+
+        def own_loop(c, carry):
+            own(c)
+            return carry
+
+        lax.fori_loop(0, nc, own_loop, 0)
+
+    @pl.when(even)
     def _():
-        pl.semaphore_wait(gate, 1)
-
-    own(None)
-
-    def own_loop(c, carry):
-        own(c)
+        own_all()
+
+    ones = jnp.ones((8, width), bf16)
+
+    def row_sum(rows):
+        return lax.dot_general(
+            ones, rows, (((1,), (1,)), ((), ())), preferred_element_type=f32
+        )
+
+    def count(c, carry):
+        part = gat[z, crows(c, HDR), :]
+        square = part.astype(f32) * part.astype(f32)
+        high = square.astype(bf16)
+        low = (square - high.astype(f32)).astype(bf16)
+        lanes = pl.ds(pl.multiple_of(c * chunk, 128), chunk)
+        sums[z, 0:8, lanes] = row_sum(part)
+        sums[z, 8:16, lanes] = row_sum(high) + row_sum(low)
         return carry
 
-    lax.fori_loop(0, nc, own_loop, 0)
+    lax.fori_loop(0, nc, count, 0)
+
+    def sx(d):
+        return pltpu.make_async_remote_copy(
+            src_ref=sums.at[z], dst_ref=sums.at[z],
+            send_sem=s_send.at[d], recv_sem=s_recv.at[d],
+            device_id={"tensor": lax.rem(z + d, n)}, device_id_type=pl.DeviceIdType.MESH,
+        )
+
+    for d in range(1, n):
+        sx(d).start()
 
     def drain_gather():
         def one(c, carry):
@@ -150,63 +181,88 @@
             def _():
                 ag(s, c, 1).wait_send()
 
-    for d in range(1, n):
-        forward(d, None)
-        if d < n - 1:
-
-            def forward_loop(c, carry, d=d):
-                forward(d, c)
-                return carry
-
-            lax.fori_loop(0, nc, forward_loop, 0)
-
     for load in loads:
         load.wait()
-
-    def project(c, carry):
-        forward(n - 1, c)
-
-        @pl.when((c == nc - 1) & even)
-        def _():
-            drain_gather()
-            pl.semaphore_signal(
-                gate, inc=1, device_id={"tm": partners[0][0]},
-                device_id_type=pl.DeviceIdType.MESH,
-            )
-
-        rows = crows(c, HDR)
-        total = jnp.zeros((chunk, 1), f32)
-        square = jnp.zeros((chunk, 1), f32)
-        for s in range(n):
-            part = gat[s, rows, :].astype(f32)
-            total += jnp.sum(part, axis=1, keepdims=True)
-            square += jnp.sum(part * part, axis=1, keepdims=True)
-        mean = total * (1.0 / full)
-        var = square * (1.0 / full) - mean * mean
-        rstd = lax.rsqrt(var + epsilon)
-        for s in range(n):
-            head_rows = gat[s, pl.ds(0, HDR), :].astype(f32)
-            part = gat[s, rows, :].astype(f32)
-            modb[:, s * width : (s + 1) * width] = (
-                (part - mean) * rstd * (1.0 + head_rows[1:2]) + head_rows[0:1]
-            ).astype(bf16)
+    for d in range(1, n):
+        sx(d).wait()
+
+    total = sums[0]
+    for s in range(1, n):
+        total = total + sums[s]
+    mean_row = total[0:8] * (1.0 / full)
+    stat[0:8, :] = mean_row
+    stat[8:16, :] = lax.rsqrt(total[8:16] * (1.0 / full) - mean_row * mean_row + epsilon)
+
+    def accumulate(s, c, begin):
+        lanes = pl.ds(pl.multiple_of(c * chunk, 128), chunk)
+        columns = jnp.transpose(stat[:, lanes])
+        head_rows = gat[s, pl.ds(0, HDR), :].astype(f32)
+        part = gat[s, crows(c, HDR), :].astype(f32)
+        rows = (
+            (part - columns[:, 0:1]) * columns[:, 8:9] * (1.0 + head_rows[1:2]) + head_rows[0:1]
+        ).astype(bf16)
         for j in range(3):
-            out = jnp.dot(
-                modb[...], wbuf[j * full : (j + 1) * full, :], preferred_element_type=f32
-            )
-            if j == 2:
-                qkv[j, crows(c), :] = out.astype(bf16)
+            cols = slice(j * width, (j + 1) * width)
+            depth = pl.ds(pl.multiple_of(j * full + s * width, 128), width)
+            out = jnp.dot(rows, wbuf[depth, :], preferred_element_type=f32)
+            if begin:
+                acc[crows(c), cols] = out
             else:
-                for h in range(heads):
-                    cols = slice(h * HEAD, (h + 1) * HEAD)
-                    vec = out[:, cols]
+                acc[crows(c), cols] += out
+
+    def own_part(c, carry):
+        accumulate(z, c, True)
+        return carry
+
+    lax.fori_loop(0, nc, own_part, 0)
+
+    @pl.when(jnp.logical_not(even))
+    def _():
+        pl.semaphore_wait(gate, 1)
+        own_all()
+
+    def finish(c):
+        for j in range(3):
+            for h in range(heads):
+                cols = slice(h * HEAD, (h + 1) * HEAD)
+                vec = acc[crows(c), j * width + h * HEAD : j * width + (h + 1) * HEAD]
+                if j < 2:
                     power = jnp.mean(vec * vec, axis=1, keepdims=True)
-                    qkv[j, crows(c), cols] = (
-                        vec * lax.rsqrt(power + epsilon) * gains_ref[j : j + 1, cols]
-                    ).astype(bf16)
+                    vec = vec * lax.rsqrt(power + epsilon) * gains_ref[j : j + 1, cols]
+                qkv[j, crows(c), cols] = vec.astype(bf16)
+
+    def distance(d, carry):
+        forward(d, None)
+
+        def one(c, carry):
+            forward(d, c)
+
+            @pl.when((d == n - 1) & (c == 0) & even)
+            def _():
+                drain_gather()
+                pl.semaphore_signal(
+                    gate, inc=1, device_id={"tm": partners[0][0]},
+                    device_id_type=pl.DeviceIdType.MESH,
+                )
+
+            @pl.when(z >= d)
+            def _():
+                accumulate(z - d, c, False)
+
+            @pl.when(z + d < n)
+            def _():
+                accumulate(z + d, c, False)
+
+            @pl.when(d == n - 1)
+            def _():
+                finish(c)
+
+            return carry
+
+        lax.fori_loop(0, nc, one, 0)
         return carry
 
-    lax.fori_loop(0, nc, project, 0)
+    lax.fori_loop(1, n, distance, 0)
 
     def prow(t, c):
         return pl.ds(pl.multiple_of(t * length + c * sub, 16), sub)
@@ -225,7 +281,7 @@
 
     def tx(k, c):
         return pltpu.make_async_remote_copy(
-            src_ref=tsend.at[k, srows(c)], dst_ref=trecv.at[k, srows(c)],
+            src_ref=wbuf.at[prow(n + k, c)], dst_ref=trecv.at[k, srows(c)],
             send_sem=t_send.at[k, c], recv_sem=t_recv.at[k, c],
             device_id={"tm": partners[k][0]}, device_id_type=pl.DeviceIdType.MESH,
         )
@@ -321,7 +377,7 @@
         vel_ref[rows, :] = velocity.astype(bf16)
         start = jnp.where(first, state, jnp.zeros_like(state))
         upd_ref[rows, :] = start
-        tsend[0, rows, :] = (
+        wbuf[prow(n, c), :] = (
             noise[rows, :].astype(f32) - step_ref[0] * velocity + start
         ).astype(bf16)
         tx(0, c).start()
@@ -331,7 +387,9 @@
         tx(k, c).wait_recv()
         arrived = trecv[k, rows, :].astype(f32)
         if k < levels - 1:
-            tsend[k + 1, rows, :] = (tsend[k, rows, :].astype(f32) + arrived).astype(bf16)
+            wbuf[prow(n + k + 1, c), :] = (
+                wbuf[prow(n + k, c), :].astype(f32) + arrived
+            ).astype(bf16)
             tx(k + 1, c).start()
         keep = partners[k][1].astype(f32)
         now = upd_ref[rows, :] + keep * arrived
@@ -435,17 +493,18 @@
         out_specs=(vmem, vmem, vmem),
         scratch_shapes=[
             pltpu.VMEM((n, HDR + length, width), bf16),
-            pltpu.VMEM((3 * full, width), bf16),
+            pltpu.VMEM((max(3 * full, (n + levels) * length), width), bf16),
             pltpu.VMEM((width, full), bf16),
             pltpu.VMEM((3, length, width), bf16),
             pltpu.VMEM((n + 1, length, width), bf16),
             pltpu.VMEM((levels, length, width), bf16),
-            pltpu.VMEM((levels, length, width), bf16),
             pltpu.VMEM((length, width), bf16),
-            pltpu.VMEM((chunk, full), bf16),
+            pltpu.VMEM((length, 3 * width), f32),
             pltpu.VMEM((chunk, width), bf16),
             pltpu.VMEM((8, width), f32),
             pltpu.VMEM((n, 8, 128), f32),
+            pltpu.VMEM((n, 16, length), f32),
+            pltpu.VMEM((16, length), f32),
             dma((5,)),
             dma((2, n, nc + 1)),
             dma((n, nc + 1)),
@@ -453,6 +512,8 @@
             dma((2, n, ns)),
             dma((levels, ns)),
             dma((levels, ns)),
+            dma((n,)),
+            dma((n,)),
             dma((n,)),
             dma((n,)),
             pltpu.SemaphoreType.REGULAR,

time: 283 us -> 290 us (1.025)
  Pallas kernels: 271 us -> 279 us
    pallas_call x1, Pallas kernels: 271 us -> 279 us  [body(): pl.pallas_call(functools.partial(kernel, n, tm_size, chunk), out_shape=(j...]
where the time goes in v3:
time: 290 us
  Pallas kernels  279 us (96%)
  local copies, waits for them, and re-layouts  7.48 us (3%)
  between operations  3.15 us (1%)
    pallas_call x1, Pallas kernels, body(): pl.pallas_call(functools.partial(kernel, n, tm_size, chunk), out_shape=(j...  279 us

profile of v3, /device:TPU:0, one launch (start us, length us, event | category | flops | bytes accessed | tf_op | source)
XLA Modules:
  0.0 289.9 jit_solution(4809604087502416825)
XLA Ops:
  0.6 0.0 copy-start
  1.3 1.2 dynamic_slice.5.step_ref
  2.6 0.0 copy-done
  2.6 0.6 pad_convert_fusion.mod_ref
  3.2 278.6 %shard_map.103 = (f32[1024,768]{1,0:T(8,128)}, bf16[1024,768]{1,0:T(8,128)(2,1)}, f32[8,128]{1,0:T(8,128)}) custom-call(f32[1024,768]{1,0:T(8,128)} %bitcast.13, bf16[1024,768]{1,0:T(8,128)(2,1)} %bitcast.15, bf16[3,3072,768]{2,1,0:T(8,128)(2,1)} %bitcast.11, f32[2,768]{1,0:T(2,128)} %gains_ref.1, bf16[768,3072]{1,0:T(8,128)(2,1)} %wo_hbm.1, ...), custom_call_target="tpu_custom_call" | custom-call | tf_op jit(solution)/shard_map/pallas_call | solution.py:485
  281.9 1.2 slice.3
  283.7 0.0 copy-start.1
  283.7 3.9 %copy.17 = f32[1,1024,768]{2,1,0:T(8,128)} copy(f32[1,1024,768]{2,1,0:T(8,128)} %bitcast.12) | data formatting | bytes 6291456
  287.6 0.0 copy-done.1
  287.6 1.1 copy.18
  (2 shorter events, 0.0 us)
Async XLA Ops:
  0.6 2.0 copy-start
  283.7 3.9 %copy-start.1 = (bf16[1024,768]{1,0:T(8,128)(2,1)S(1)}, bf16[1024,768]{1,0:T(8,128)(2,1)}, u32[]{:S(2)}) copy-start(bf16[1024,768]{1,0:T(8,128)(2,1)} %get-tuple-element.7) | copy-start | bytes 4718596

commit v4 on v3

--- a/solution.py
+++ b/solution.py
@@ -19,11 +19,11 @@
 
 def kernel(
     n, tm_size, chunk,
-    x_ref, noise_hbm, w_hbm, gains_ref, wo_hbm, mod_ref, step_ref,
+    x_ref, noise_hbm, w_hbm, gains_ref, wo_hbm, mod_ref,
     upd_ref, vel_ref, err_ref,
     gat, wbuf, wo, qkv, rbuf, trecv, noise, acc, att, erracc, ebuf, sums, stat,
     load_sem, ag_send, ag_recv, rs_send, rs_recv, t_send, t_recv, e_send, e_recv,
-    s_send, s_recv, gate,
+    s_send, s_recv,
 ):
     z = lax.axis_index("tensor")
     slot = lax.axis_index("tm")
@@ -119,8 +119,6 @@
             def _():
                 ag(z + d, c, 1).start()
 
-    even = partners[0][1] == 0
-
     def own_all():
         own(None)
 
@@ -130,9 +128,7 @@
 
         lax.fori_loop(0, nc, own_loop, 0)
 
-    @pl.when(even)
-    def _():
-        own_all()
+    own_all()
 
     ones = jnp.ones((8, width), bf16)
 
@@ -216,11 +212,6 @@
 
     lax.fori_loop(0, nc, own_part, 0)
 
-    @pl.when(jnp.logical_not(even))
-    def _():
-        pl.semaphore_wait(gate, 1)
-        own_all()
-
     def finish(c):
         for j in range(3):
             for h in range(heads):
@@ -236,14 +227,6 @@
 
         def one(c, carry):
             forward(d, c)
-
-            @pl.when((d == n - 1) & (c == 0) & even)
-            def _():
-                drain_gather()
-                pl.semaphore_signal(
-                    gate, inc=1, device_id={"tm": partners[0][0]},
-                    device_id_type=pl.DeviceIdType.MESH,
-                )
 
             @pl.when(z >= d)
             def _():
@@ -378,7 +361,7 @@
         start = jnp.where(first, state, jnp.zeros_like(state))
         upd_ref[rows, :] = start
         wbuf[prow(n, c), :] = (
-            noise[rows, :].astype(f32) - step_ref[0] * velocity + start
+            noise[rows, :].astype(f32) - mod_ref[3:4, :] * velocity + start
         ).astype(bf16)
         tx(0, c).start()
 
@@ -437,9 +420,7 @@
     for d in range(1, n):
         ex(d).start()
 
-    @pl.when(jnp.logical_not(even))
-    def _():
-        drain_gather()
+    drain_gather()
 
     def drain(c, carry):
         for s in range(n):
@@ -461,7 +442,7 @@
     total = ebuf[0]
     for s in range(1, n):
         total = total + ebuf[s]
-    err_ref[...] = total
+    err_ref[0] = jnp.max(total) * (1.0 / (length * full))
 
 
 def body(latents, noise, qkv_weight, qk_gains, out_weight, modulation, step_sizes, window_start):
@@ -473,8 +454,10 @@
     mod_rows = lax.dynamic_index_in_dim(
         modulation.transpose(1, 0, 2), offset, 1, keepdims=False
     ).astype(f32)
-    mod_rows = jnp.pad(mod_rows, ((0, HDR - 3), (0, 0)))
-    step_size = lax.dynamic_slice_in_dim(step_sizes, offset, 1, 0)
+    step_size = lax.dynamic_index_in_dim(step_sizes, offset, 0, keepdims=False)
+    mod_rows = jnp.concatenate(
+        [mod_rows, jnp.full((1, width), step_size), jnp.zeros((HDR - 4, width), f32)]
+    )
     chunk = CHUNK
     nc = length // chunk
     ns = nc * SPLIT
@@ -487,10 +470,10 @@
         out_shape=(
             jax.ShapeDtypeStruct((length, width), f32),
             jax.ShapeDtypeStruct((length, width), bf16),
-            jax.ShapeDtypeStruct((8, 128), f32),
+            jax.ShapeDtypeStruct((1,), f32),
         ),
-        in_specs=[vmem, hbm, hbm, vmem, hbm, vmem, pl.BlockSpec(memory_space=pltpu.SMEM)],
-        out_specs=(vmem, vmem, vmem),
+        in_specs=[vmem, hbm, hbm, vmem, hbm, vmem],
+        out_specs=(vmem, vmem, pl.BlockSpec(memory_space=pltpu.SMEM)),
         scratch_shapes=[
             pltpu.VMEM((n, HDR + length, width), bf16),
             pltpu.VMEM((max(3 * full, (n + levels) * length), width), bf16),
@@ -516,16 +499,15 @@
             dma((n,)),
             dma((n,)),
             dma((n,)),
-            pltpu.SemaphoreType.REGULAR,
         ],
         compiler_params=pltpu.CompilerParams(
             collective_id=0, has_side_effects=True, vmem_limit_bytes=62 * 2**20
         ),
     )(
         latents[0], noise[0], qkv_weight.transpose(1, 0, 2), qk_gains, out_weight,
-        mod_rows, step_size,
+        mod_rows,
     )
-    return (updated[None], velocity[None], err[0, :1] / (length * full))
+    return (updated[None], velocity[None], err)
 
 
 def solution(mesh):

time: 290 us -> 302 us (1.041)
  Pallas kernels: 279 us -> 291 us
    pallas_call x1, Pallas kernels: 279 us -> 291 us  [body(): pl.pallas_call(functools.partial(kernel, n, tm_size, chunk), out_shape=(j...]
where the time goes in v4:
time: 302 us
  Pallas kernels  291 us (96%)
  local copies, waits for them, and re-layouts  7.08 us (2%)
  between operations  3.06 us (1%)
    pallas_call x1, Pallas kernels, body(): pl.pallas_call(functools.partial(kernel, n, tm_size, chunk), out_shape=(j...  291 us

profile of v4, /device:TPU:0, one launch (start us, length us, event | category | flops | bytes accessed | tf_op | source)
XLA Modules:
  0.0 302.1 jit_solution(323104841555627214)
XLA Ops:
  0.6 0.0 copy-start
  1.3 1.2 dynamic_slice.6
  2.6 0.7 pad.1.clone
  3.3 0.1 pad.2.clone
  3.4 0.0 copy-done
  3.4 0.7 maximum_maximum_fusion.mod_ref
  4.1 291.3 %shard_map.103 = (f32[1024,768]{1,0:T(8,128)}, bf16[1024,768]{1,0:T(8,128)(2,1)}, f32[1]{0:T(128)}) custom-call(f32[1024,768]{1,0:T(8,128)} %bitcast.15, bf16[1024,768]{1,0:T(8,128)(2,1)} %bitcast.16, bf16[3,3072,768]{2,1,0:T(8,128)(2,1)} %bitcast.13, f32[2,768]{1,0:T(2,128)} %gains_ref.1, bf16[768,3072]{1,0:T(8,128)(2,1)} %wo_hbm.1, ...), custom_call_target="tpu_custom_call" | custom-call | tf_op jit(solution)/shard_map/pallas_call | solution.py:468
  295.4 0.0 copy-start.1
  295.4 3.9 %copy.20 = f32[1,1024,768]{2,1,0:T(8,128)} copy(f32[1,1024,768]{2,1,0:T(8,128)} %bitcast.14) | data formatting | bytes 6291456
  299.3 0.0 copy-done.1
  299.3 1.1 copy.21
  (3 shorter events, 0.0 us)
Async XLA Ops:
  0.6 2.8 copy-start
  295.4 3.9 %copy-start.1 = (bf16[1024,768]{1,0:T(8,128)(2,1)S(1)}, bf16[1024,768]{1,0:T(8,128)(2,1)}, u32[]{:S(2)}) copy-start(bf16[1024,768]{1,0:T(8,128)(2,1)} %get-tuple-element.7) | copy-start | bytes 4718596

commit v5 on v4

--- a/solution.py
+++ b/solution.py
@@ -80,8 +80,17 @@
     lax.fori_loop(0, nc, cast, 0)
     pl.semaphore_wait(barrier, n - 1 + levels)
 
-    right = jnp.minimum(z + 1, n - 1)
-    left = jnp.maximum(z - 1, 0)
+    right, left = lax.rem(z + 1, n), lax.rem(z + n - 1, n)
+    half = n // 2
+
+    def away(way, k):
+        return lax.rem(z + k, n) if way == 0 else lax.rem(z + n - k, n)
+
+    def reach(way, c, count):
+        if c is None:
+            return half - way
+        early = c < count // 2
+        return jnp.where(early, half - way, half - 1 + way)
 
     def ag(s, c, way):
         rows = pl.ds(0, HDR) if c is None else crows(c, HDR)
@@ -94,30 +103,20 @@
         )
 
     def own(c):
-        @pl.when(z < n - 1)
-        def _():
-            ag(z, c, 0).start()
-
-        @pl.when(z > 0)
-        def _():
-            ag(z, c, 1).start()
+        ag(z, c, 0).start()
+        ag(z, c, 1).start()
 
     def forward(d, c):
-        @pl.when(z >= d)
-        def _():
-            ag(z - d, c, 0).wait_recv()
-
-            @pl.when(z < n - 1)
-            def _():
-                ag(z - d, c, 0).start()
-
-        @pl.when(z + d < n)
-        def _():
-            ag(z + d, c, 1).wait_recv()
-
-            @pl.when(z > 0)
-            def _():
-                ag(z + d, c, 1).start()
+        for way in (0, 1):
+            s = away(1 - way, d)
+
+            @pl.when(d <= reach(way, c, nc))
+            def _(s=s, way=way):
+                ag(s, c, way).wait_recv()
+
+                @pl.when(d < reach(way, c, nc))
+                def _():
+                    ag(s, c, way).start()
 
     def own_all():
         own(None)
@@ -168,14 +167,11 @@
         lax.fori_loop(0, nc, one, 0)
 
     def drain_one(c):
-        for s in range(n):
-            @pl.when((z < n - 1) & (s <= z))
-            def _():
-                ag(s, c, 0).wait_send()
-
-            @pl.when((z > 0) & (s >= z))
-            def _():
-                ag(s, c, 1).wait_send()
+        for way in (0, 1):
+            for e in range(half):
+                @pl.when(e < reach(way, c, nc))
+                def _(way=way, e=e):
+                    ag(away(1 - way, e), c, way).wait_send()
 
     for load in loads:
         load.wait()
@@ -228,15 +224,12 @@
         def one(c, carry):
             forward(d, c)
 
-            @pl.when(z >= d)
-            def _():
-                accumulate(z - d, c, False)
-
-            @pl.when(z + d < n)
-            def _():
-                accumulate(z + d, c, False)
-
-            @pl.when(d == n - 1)
+            for way in (0, 1):
+                @pl.when(d <= reach(way, c, nc))
+                def _(way=way):
+                    accumulate(away(1 - way, d), c, False)
+
+            @pl.when(d == half)
             def _():
                 finish(c)
 
@@ -245,7 +238,7 @@
         lax.fori_loop(0, nc, one, 0)
         return carry
 
-    lax.fori_loop(1, n, distance, 0)
+    lax.fori_loop(1, half + 1, distance, 0)
 
     def prow(t, c):
         return pl.ds(pl.multiple_of(t * length + c * sub, 16), sub)
@@ -254,7 +247,7 @@
         if way == 0:
             place = t
         else:
-            place = jnp.where(t == z - 1, n, t)
+            place = jnp.where(t == left, n, t)
         return pltpu.make_async_remote_copy(
             src_ref=wbuf.at[prow(t, c)], dst_ref=rbuf.at[place, srows(c)],
             send_sem=rs_send.at[way, t, c], recv_sem=rs_recv.at[way, t, c],
@@ -297,66 +290,40 @@
 
         lax.fori_loop(0, n, one_part, 0)
 
-        @pl.when(z == 0)
-        def _():
-            for p in range(SPLIT):
-                for t in range(n - 1, 0, -1):
-                    rs(t, c * SPLIT + p, 0).start()
-
-        @pl.when(z == n - 1)
-        def _():
-            for p in range(SPLIT):
-                for t in range(n - 1):
-                    rs(t, c * SPLIT + p, 1).start()
+        for p in range(SPLIT):
+            sc = c * SPLIT + p
+            for way in (0, 1):
+                rs(away(way, reach(way, sc, ns)), sc, way).start()
 
     def stage_join(c):
-        for t in range(n - 1, 0, -1):
-            @pl.when((z > 0) & (z < t))
-            def _():
-                rs(t, c, 0).wait_recv()
-                wbuf[prow(t, c), :] = (
-                    wbuf[prow(t, c), :].astype(f32) + rbuf[t, srows(c), :].astype(f32)
-                ).astype(bf16)
-                rs(t, c, 0).start()
-
-            u = n - 1 - t
-
-            @pl.when((z < n - 1) & (z > u))
-            def _():
-                rs(u, c, 1).wait_recv()
-                wbuf[prow(u, c), :] = (
-                    wbuf[prow(u, c), :].astype(f32) + rbuf[u, srows(c), :].astype(f32)
-                ).astype(bf16)
-                rs(u, c, 1).start()
+        for k in range(half - 1, 0, -1):
+            for way in (0, 1):
+                t = away(way, k)
+
+                @pl.when(k < reach(way, c, ns))
+                def _(t=t, way=way):
+                    rs(t, c, way).wait_recv()
+                    wbuf[prow(t, c), :] = (
+                        wbuf[prow(t, c), :].astype(f32) + rbuf[t, srows(c), :].astype(f32)
+                    ).astype(bf16)
+                    rs(t, c, way).start()
 
     def stage_velocity(c):
         rows = srows(c)
 
-        @pl.when(z > 0)
-        def _():
-            rs(z, c, 0).wait_recv()
-
-        @pl.when(z < n - 1)
-        def _():
-            pltpu.make_async_remote_copy(
-                src_ref=wbuf.at[prow(z, c)], dst_ref=rbuf.at[n, rows],
-                send_sem=rs_send.at[1, z, c], recv_sem=rs_recv.at[1, z, c],
-                device_id={"tensor": right}, device_id_type=pl.DeviceIdType.MESH,
-            ).wait_recv()
-
-        branch = wbuf[prow(z, c), :].astype(f32)
-        upd_ref[rows, :] = branch
-
-        @pl.when(z > 0)
-        def _():
-            upd_ref[rows, :] = upd_ref[rows, :] + rbuf[z, rows, :].astype(f32)
-
-        @pl.when(z < n - 1)
-        def _():
-            upd_ref[rows, :] = upd_ref[rows, :] + rbuf[n, rows, :].astype(f32)
-
+        rs(z, c, 0).wait_recv()
+        pltpu.make_async_remote_copy(
+            src_ref=wbuf.at[prow(z, c)], dst_ref=rbuf.at[n, rows],
+            send_sem=rs_send.at[1, z, c], recv_sem=rs_recv.at[1, z, c],
+            device_id={"tensor": left}, device_id_type=pl.DeviceIdType.MESH,
+        ).wait_recv()
+        branch = (
+            wbuf[prow(z, c), :].astype(f32)
+            + rbuf[z, rows, :].astype(f32)
+            + rbuf[n, rows, :].astype(f32)
+        )
         state = x_ref[rows, :]
-        velocity = state + mod_ref[2:3, :] * upd_ref[rows, :]
+        velocity = state + mod_ref[2:3, :] * branch
         vel_ref[rows, :] = velocity.astype(bf16)
         start = jnp.where(first, state, jnp.zeros_like(state))
         upd_ref[rows, :] = start
@@ -423,14 +390,11 @@
     drain_gather()
 
     def drain(c, carry):
-        for s in range(n):
-            @pl.when(z < s)
-            def _():
-                rs(s, c, 0).wait_send()
-
-            @pl.when(z > s)
-            def _():
-                rs(s, c, 1).wait_send()
+        for way in (0, 1):
+            for k in range(1, half + 1):
+                @pl.when(k <= reach(way, c, ns))
+                def _(way=way, k=k):
+                    rs(away(way, k), c, way).wait_send()
 
         for k in range(levels):
             tx(k, c).wait_send()

time: 302 us -> 276 us (0.914)
  Pallas kernels: 291 us -> 264 us
    pallas_call x1, Pallas kernels: 291 us -> 264 us  [body(): pl.pallas_call(functools.partial(kernel, n, tm_size, chunk), out_shape=(j...]
where the time goes in v5:
time: 276 us; the launch traced here: 275 us
  Pallas kernels  264 us (96%)
  local copies, waits for them, and re-layouts  7.08 us (3%)
  between operations  3.06 us (1%)
    pallas_call x1, Pallas kernels, body(): pl.pallas_call(functools.partial(kernel, n, tm_size, chunk), out_shape=(j...  264 us

profile of v5, /device:TPU:0, one launch (start us, length us, event | category | flops | bytes accessed | tf_op | source)
XLA Modules:
  0.0 275.3 jit_solution(9644523693236912503)
XLA Ops:
  0.6 0.0 copy-start
  1.3 1.2 dynamic_slice.6
  2.6 0.7 pad.1.clone
  3.3 0.1 pad.2.clone
  3.4 0.0 copy-done
  3.4 0.7 maximum_maximum_fusion.mod_ref
  4.1 264.5 %shard_map.103 = (f32[1024,768]{1,0:T(8,128)}, bf16[1024,768]{1,0:T(8,128)(2,1)}, f32[1]{0:T(128)}) custom-call(f32[1024,768]{1,0:T(8,128)} %bitcast.15, bf16[1024,768]{1,0:T(8,128)(2,1)} %bitcast.16, bf16[3,3072,768]{2,1,0:T(8,128)(2,1)} %bitcast.13, f32[2,768]{1,0:T(2,128)} %gains_ref.1, bf16[768,3072]{1,0:T(8,128)(2,1)} %wo_hbm.1, ...), custom_call_target="tpu_custom_call" | custom-call | tf_op jit(solution)/shard_map/pallas_call | solution.py:432
  268.6 0.0 copy-start.1
  268.6 3.9 %copy.20 = f32[1,1024,768]{2,1,0:T(8,128)} copy(f32[1,1024,768]{2,1,0:T(8,128)} %bitcast.14) | data formatting | bytes 6291456
  272.5 0.0 copy-done.1
  272.5 1.1 copy.21
  (3 shorter events, 0.0 us)
Async XLA Ops:
  0.6 2.8 %copy-start = (bf16[64,3,768]{2,0,1:T(8,128)(2,1)S(1)}, bf16[64,3,768]{2,0,1:T(8,128)(2,1)}, u32[]{:S(2)}) copy-start(bf16[64,3,768]{2,0,1:T(8,128)(2,1)} %param.13) | copy-start | bytes 884740
  268.6 3.9 %copy-start.1 = (bf16[1024,768]{1,0:T(8,128)(2,1)S(1)}, bf16[1024,768]{1,0:T(8,128)(2,1)}, u32[]{:S(2)}) copy-start(bf16[1024,768]{1,0:T(8,128)(2,1)} %get-tuple-element.7) | copy-start | bytes 4718596

commit v6 on v5

--- a/solution.py
+++ b/solution.py
@@ -21,7 +21,7 @@
     n, tm_size, chunk,
     x_ref, noise_hbm, w_hbm, gains_ref, wo_hbm, mod_ref,
     upd_ref, vel_ref, err_ref,
-    gat, wbuf, wo, qkv, rbuf, trecv, noise, acc, att, erracc, ebuf, sums, stat,
+    gat, wbuf, wo, qs, kt, vs, rbuf, trecv, noise, acc, att, erracc, ebuf, sums, stat,
     load_sem, ag_send, ag_recv, rs_send, rs_recv, t_send, t_recv, e_send, e_recv,
     s_send, s_recv,
 ):
@@ -216,7 +216,16 @@
                 if j < 2:
                     power = jnp.mean(vec * vec, axis=1, keepdims=True)
                     vec = vec * lax.rsqrt(power + epsilon) * gains_ref[j : j + 1, cols]
-                qkv[j, crows(c), cols] = vec.astype(bf16)
+                if j == 0:
+                    qs[crows(c), cols] = vec.astype(bf16)
+                elif j == 1:
+                    lanes = pl.ds(pl.multiple_of(c * chunk, 128), chunk)
+                    kt[cols, lanes] = jnp.transpose(vec).astype(bf16)
+                else:
+                    vs[crows(c), 2 * h * HEAD : (2 * h + 1) * HEAD] = vec.astype(bf16)
+                    vs[crows(c), (2 * h + 1) * HEAD : (2 * h + 2) * HEAD] = jnp.ones(
+                        (chunk, HEAD), bf16
+                    )
 
     def distance(d, carry):
         forward(d, None)
@@ -267,15 +276,12 @@
     def stage_attend(c):
         def one_head(h, carry):
             cols = pl.ds(pl.multiple_of(h * HEAD, HEAD), HEAD)
-            scores = lax.dot_general(
-                qkv[0, crows(c), cols], qkv[1, :, cols], (((1,), (1,)), ((), ())),
-                preferred_element_type=f32,
-            )
+            wide = pl.ds(pl.multiple_of(h * 2 * HEAD, 2 * HEAD), 2 * HEAD)
+            scores = jnp.dot(qs[crows(c), cols], kt[cols, :], preferred_element_type=f32)
             top = jnp.max(scores, axis=1, keepdims=True)
-            weights = jnp.exp2((scores - top) * exponent)
-            norm = jnp.sum(weights, axis=1, keepdims=True)
-            out = jnp.dot(weights.astype(bf16), qkv[2, :, cols], preferred_element_type=f32)
-            att[:, cols] = (out / norm).astype(bf16)
+            weights = jnp.exp2((scores - top) * exponent).astype(bf16)
+            out = jnp.dot(weights, vs[:, wide], preferred_element_type=f32)
+            att[:, cols] = (out[:, :HEAD] / out[:, HEAD:]).astype(bf16)
             return carry
 
         lax.fori_loop(0, heads, one_head, 0, unroll=3)
@@ -351,7 +357,7 @@
             )
 
     erracc[...] = jnp.zeros_like(erracc)
-    lag = 5
+    lag = 3
 
     def turn(i, carry):
         @pl.when((i < ns) & (lax.rem(i, SPLIT) == 0))
@@ -442,7 +448,9 @@
             pltpu.VMEM((n, HDR + length, width), bf16),
             pltpu.VMEM((max(3 * full, (n + levels) * length), width), bf16),
             pltpu.VMEM((width, full), bf16),
-            pltpu.VMEM((3, length, width), bf16),
+            pltpu.VMEM((length, width), bf16),
+            pltpu.VMEM((width, length), bf16),
+            pltpu.VMEM((length, 2 * width), bf16),
             pltpu.VMEM((n + 1, length, width), bf16),
             pltpu.VMEM((levels, length, width), bf16),
             pltpu.VMEM((length, width), bf16),

time: 276 us -> 271 us (0.982)
  Pallas kernels: 264 us -> 260 us
    pallas_call x1, Pallas kernels: 264 us -> 260 us  [body(): pl.pallas_call(functools.partial(kernel, n, tm_size, chunk), out_shape=(j...]
where the time goes in v6:
time: 271 us
  Pallas kernels  260 us (96%)
  local copies, waits for them, and re-layouts  7.08 us (3%)
  between operations  3.06 us (1%)
    pallas_call x1, Pallas kernels, body(): pl.pallas_call(functools.partial(kernel, n, tm_size, chunk), out_shape=(j...  260 us

profile of v6, /device:TPU:0, one launch (start us, length us, event | category | flops | bytes accessed | tf_op | source)
XLA Modules:
  0.0 270.8 jit_solution(1709358386825460892)
XLA Ops:
  0.6 0.0 copy-start
  1.3 1.2 dynamic_slice.6
  2.6 0.7 pad.1.clone
  3.3 0.1 pad.2.clone
  3.4 0.0 copy-done
  3.4 0.7 maximum_maximum_fusion.mod_ref
  4.1 260.0 %shard_map.103 = (f32[1024,768]{1,0:T(8,128)}, bf16[1024,768]{1,0:T(8,128)(2,1)}, f32[1]{0:T(128)}) custom-call(f32[1024,768]{1,0:T(8,128)} %bitcast.15, bf16[1024,768]{1,0:T(8,128)(2,1)} %bitcast.16, bf16[3,3072,768]{2,1,0:T(8,128)(2,1)} %bitcast.13, f32[2,768]{1,0:T(2,128)} %gains_ref.1, bf16[768,3072]{1,0:T(8,128)(2,1)} %wo_hbm.1, ...), custom_call_target="tpu_custom_call" | custom-call | tf_op jit(solution)/shard_map/pallas_call | solution.py:438
  264.1 0.0 copy-start.1
  264.1 3.9 %copy.20 = f32[1,1024,768]{2,1,0:T(8,128)} copy(f32[1,1024,768]{2,1,0:T(8,128)} %bitcast.14) | data formatting | bytes 6291456
  268.0 0.0 copy-done.1
  268.0 1.1 copy.21
  (3 shorter events, 0.0 us)
Async XLA Ops:
  0.6 2.8 %copy-start = (bf16[64,3,768]{2,0,1:T(8,128)(2,1)S(1)}, bf16[64,3,768]{2,0,1:T(8,128)(2,1)}, u32[]{:S(2)}) copy-start(bf16[64,3,768]{2,0,1:T(8,128)(2,1)} %param.13) | copy-start | bytes 884740
  264.1 3.9 %copy-start.1 = (bf16[1024,768]{1,0:T(8,128)(2,1)S(1)}, bf16[1024,768]{1,0:T(8,128)(2,1)}, u32[]{:S(2)}) copy-start(bf16[1024,768]{1,0:T(8,128)(2,1)} %get-tuple-element.7) | copy-start | bytes 4718596
